TPU v7x, 128 devices: a whole 4x4x4 slice. The times are simulated.
128 devices in a mesh: row: 8 (over y, core), col: 16 (over x, z).
Axes of the slice: x: 4, y: 4, z: 4, core: 2. Of those that a mesh axis runs over, the one named last changes fastest.
Arguments:
- transition: bfloat16 [12288, 12288], P('row', 'col'), may hold values from 0 to 36.084392, as said below
- tile_pattern: int32 [96, 96], P('row', 'col'), may hold values from 0 to 1, as said below
- kept_tiles: int32 [96, 48], P('row', 'col'), may hold values from 0 to 1, as said below
Outputs:
- next_panel: float32 [12288, 6144], P('row', 'col')
- chaos: float32 [], replicated
Inputs may be any that keep to these rules, and one draw needn't show every extreme that they name: `tile_pattern`: each device's block of 12 x 6 tiles holds at most 36 nonzero tiles, and some block holds exactly 36. Every diagonal tile is nonzero. `kept_tiles`: for panel tile column p, the tile in tile row (p // 3) * 6 + p % 3 is always kept. `transition`: all entries are positive.
All inputs are finite; a program needn't handle non-finite values.
Results may differ from a plain program's by a relative error of at most 0.0003.
Values may be sent and summed in bfloat16 or wider, within the bound.
A program may use at most 128 MiB of HBM per device.

v0:
```python
import jax
import jax.numpy as jnp
from jax import lax
from jax.sharding import PartitionSpec as P


def expand_tiles(tile_mask, tile_size):
    return jnp.repeat(jnp.repeat(tile_mask, tile_size, axis=0), tile_size, axis=1)


def body(transition, tile_pattern, kept_tiles):
    row_tiles, col_tiles = tile_pattern.shape
    tile_size = transition.shape[0] // row_tiles
    panel_cols = kept_tiles.shape[1]
    width = panel_cols * tile_size
    masked = transition * expand_tiles(tile_pattern, tile_size).astype(jnp.bfloat16)
    own_panel = masked[:, :width]
    column_panel = lax.all_gather(own_panel, "row", axis=0, tiled=True)
    product = jnp.dot(
        lax.all_gather(masked, "col", axis=1, tiled=True),
        column_panel,
        preferred_element_type=jnp.float32,
    )
    pruned = product * expand_tiles(kept_tiles, tile_size).astype(jnp.float32)
    inflated = pruned * pruned
    col_sums, squares = lax.psum(
        (jnp.sum(inflated, axis=0), jnp.sum(inflated * inflated, axis=0)), "row"
    )
    normalized = inflated / col_sums
    spread = squares / (col_sums * col_sums)
    node_count = transition.shape[0] * lax.axis_size("row")
    col_peaks = lax.pmax(jnp.max(inflated, axis=0), "row")
    local_max = jnp.max(col_peaks / col_sums - spread)
    chaos_value = lax.pmax(local_max, "col")
    return (normalized * node_count, chaos_value * node_count)


def solution(mesh):
    placed = (P("row", "col"), P("row", "col"), P("row", "col"))
    return jax.shard_map(
        body, mesh=mesh, in_specs=placed, out_specs=(P("row", "col"), P()), check_vma=False
    )
```

profile of v0, /device:TPU:0, one launch (start us, length us, event | category | flops | bytes accessed | tf_op | source)
XLA Modules:
  0.0 397.1 jit_solution(11973173878418087578)
XLA Ops:
  7.2 0.0 all-gather.5.cloned.1.call-start
  7.2 0.7 convert_element_type.22
  7.9 0.1 broadcast_bitcast_fusion.1
  8.0 4.3 %copy.7 = bf16[1536,768]{0,1:T(8,128)(2,1)} copy(bf16[1536,768]{1,0:T(8,128)(2,1)} %param.3) | data formatting | bytes 4718592 | tf_op args[0]
  12.3 1.8 bitcast_multiply_fusion
  14.1 0.0 copy-start
  14.1 1.2 slice.4
  15.3 0.0 copy-start.1
  15.3 0.0 all-gather.5.cloned.1.call-update
  15.3 0.0 all-gather.3.cloned.1.call-start
  15.4 0.5 copy-done
  15.9 0.2 all-gather.3.cloned.1.call-update
  16.1 0.0 copy-done.1
  16.1 0.1 broadcast_bitcast_fusion
  16.2 0.3 broadcast_in_dim.16
  16.5 2.0 copy.8
  18.4 53.6 %all-gather.5.cloned.1.call-done = bf16[12288,384]{0,1:T(8,128)(2,1)} async-done(((bf16[1536,384]{0,1:T(8,128)(2,1)}), bf16[12288,384]{0,1:T(8,128)(2,1)}) %all-gather.5.cloned.1.call-update) | async-done | bytes 9437200 | tf_op jit(solution)/shard_map/all_gather | solution.py:18
  72.1 221.1 %all-gather.3.cloned.1.call-done = bf16[1536,12288]{0,1:T(8,128)(2,1)} async-done(((bf16[1536,768]{0,1:T(8,128)(2,1)}), bf16[1536,12288]{0,1:T(8,128)(2,1)}) %all-gather.3.cloned.1.call-update) | async-done | bytes 37748752 | tf_op jit(solution)/shard_map/all_gather | solution.py:20
  293.2 27.1 %fusion.1 = (f32[384]{0:T(512)S(1)}, f32[384]{0:T(512)S(1)}, f32[384]{0:T(512)S(1)}, f32[1536,384]{1,0:T(8,128)S(1)}) fusion(f32[1536,384]{1,0:T(8,128)} %copy.8, bf16[1536,12288]{0,1:T(8,128)(2,1)} %all-gather.3.cloned.1.call-done, bf16[12288,384]{0,1:T(8,128)(2,1)} %all-gather.5.cloned.1.call-done), kind=kOutput, calls=%fused_computation.10 | convolution fusion | flops 14499053568 | bytes 51909120 | tf_op jit(solution)/shard_map/dot_general | solution.py:19
  320.3 14.6 %pmax.14 = f32[384]{0:T(512)S(1)} all-reduce(f32[384]{0:T(512)S(1)} %get-tuple-element.2), channel_id=1, replica_groups=mesh['row'=8,'col'=16] {'row'}, use_global_device_ids=true, to_apply=%region_3.0 | all-reduce | flops 384 | bytes 3072 | tf_op jit(solution)/shard_map/pmax | solution.py:32
  334.8 12.4 %all-reduce = (f32[384]{0:T(512)S(1)}, f32[384]{0:T(512)S(1)}) all-reduce(f32[384]{0:T(512)S(1)} %get-tuple-element.4, f32[384]{0:T(512)S(1)} %get-tuple-element.3), channel_id=1, replica_groups=mesh['row'=8,'col'=16] {'row'}, use_global_device_ids=true, to_apply=%region_1.0 | all-reduce | flops 768 | bytes 6144 | tf_op jit(solution)/shard_map/psum | solution.py:26
  347.2 0.6 subtract_reduce_fusion
  347.9 39.1 %pmax.15 = f32[]{:T(128)} all-reduce(f32[]{:T(128)} %subtract_reduce_fusion), channel_id=1, replica_groups=mesh['row'=8,'col'=16] {'col'}, use_global_device_ids=true, to_apply=%region_7.0 | all-reduce | flops 1 | bytes 8 | tf_op jit(solution)/shard_map/pmax | solution.py:34
  386.9 1.6 divide_multiply_fusion
  (3 shorter events, 0.0 us)
Async XLA Ops:
  7.2 64.9 %all-gather.5.cloned.1.call-start = ((), (), s32[]{:S(2)}) async-start(), calls=%async_computation.1 | async-start | bytes 10616832 | tf_op jit(solution)/shard_map/all_gather | solution.py:18
  14.1 1.8 copy-start
  15.3 0.8 copy-start.1
  15.3 277.8 %all-gather.3.cloned.1.call-start = ((), (), s32[]{:S(2)}) async-start(), calls=%async_computation | async-start | bytes 40108032 | tf_op jit(solution)/shard_map/all_gather | solution.py:20
Sparse Core Ops, SparseCore 0:
  15.5 56.5 all-gather.4
  74.2 218.8 all-gather.2
where the time goes:
time: 397 us
  waiting for transfers between devices  275 us (69%)
  blocking collectives  66.1 us (17%)
  matrix products  27.1 us (7%)
  between operations  15.9 us (4%)
  local copies, waits for them, and re-layouts  8.34 us (2%)
  other arithmetic  4.71 us (1%)
    all_gather x1, waiting for transfers between devices, body(): lax.all_gather(masked, 'col', axis=1, tiled=True)  221 us
    all_gather x1, waiting for transfers between devices, body(): column_panel = lax.all_gather(own_panel, 'row', axis=0, tiled=True)  53.6 us
    pmax x1, blocking collectives, body(): chaos_value = lax.pmax(local_max, 'col')  39.1 us
    dot_general x1, matrix products, body(): jnp.dot(lax.all_gather(masked, 'col', axis=1, tiled=True), column_panel,...  27.1 us
    pmax x1, blocking collectives, body(): col_peaks = lax.pmax(jnp.max(inflated, axis=0), 'row')  14.6 us
    psum x1, blocking collectives, body(): lax.psum((jnp.sum(inflated, axis=0), jnp.sum(inflated * inflated, axis=0)...  12.4 us
  transfers between devices with their start and end apart: 2, of which 2 were waited for; matrix products, arithmetic and copies ran while one was open for 1% of the time, Pallas kernels for 0%

commit v1 on v0

--- a/solution.py
+++ b/solution.py
@@ -17,7 +17,9 @@
     own_panel = masked[:, :width]
     column_panel = lax.all_gather(own_panel, "row", axis=0, tiled=True)
     product = jnp.dot(
-        lax.all_gather(masked, "col", axis=1, tiled=True),
+        jnp.concatenate(
+            lax.all_to_all(jnp.stack([masked] * lax.axis_size("col")), "col", 0, 0), axis=1
+        ),
         column_panel,
         preferred_element_type=jnp.float32,
     )

time: 397 us -> 840 us (2.12)
  waiting for transfers between devices: 275 us -> 698 us
  local copies, waits for them, and re-layouts: 8.34 us -> 20.3 us
    all_to_all x0 -> x1, waiting for transfers between devices: none -> 643 us  [body(): lax.all_to_all(jnp.stack([masked] * lax.axis_size('col')), 'col', 0, 0)]
    all_gather x1 -> x0, waiting for transfers between devices: 221 us -> none  [body(): lax.all_gather(masked, 'col', axis=1, tiled=True)]
    another operation x0 -> x1, local copies, waits for them, and re-layouts: none -> 12.5 us  [body(): jnp.stack([masked] * lax.axis_size('col'))]
  transfers between devices with their start and end apart: 2 -> 2, of which waited for: 2 -> 2; matrix products, arithmetic and copies ran while one was open for 1% -> 0% of each run, Pallas kernels for 0% -> 0%
where the time goes in v1:
time: 840 us
  waiting for transfers between devices  698 us (83%)
  blocking collectives  66.4 us (8%)
  matrix products  27 us (3%)
  local copies, waits for them, and re-layouts  20.3 us (2%)
  between operations  15.9 us (2%)
    all_to_all x1, waiting for transfers between devices, body(): lax.all_to_all(jnp.stack([masked] * lax.axis_size('col')), 'col', 0, 0)  643 us
    all_gather x1, waiting for transfers between devices, body(): column_panel = lax.all_gather(own_panel, 'row', axis=0, tiled=True)  54.8 us
    pmax x1, blocking collectives, body(): chaos_value = lax.pmax(local_max, 'col')  40 us
    dot_general x1, matrix products, body(): jnp.dot(jnp.concatenate(lax.all_to_all(jnp.stack([masked] * lax.axis_size...  27 us
  transfers between devices with their start and end apart: 2, of which 2 were waited for; matrix products, arithmetic and copies ran while one was open for 0% of the time, Pallas kernels for 0%

profile of v1, /device:TPU:0, one launch (start us, length us, event | category | flops | bytes accessed | tf_op | source)
XLA Modules:
  0.0 839.8 jit_solution(2110597788260801858)
XLA Ops:
  7.2 0.0 copy-start
  7.2 4.3 copy.7
  11.4 0.0 copy-done
  11.5 0.1 broadcast_bitcast_fusion.1
  11.6 1.8 bitcast_multiply_fusion
  13.4 12.5 %stack.2 = bf16[16,1536,768]{1,2,0:T(8,128)(2,1)} broadcast(bf16[1536,768]{0,1:T(8,128)(2,1)S(1)} %bitcast_multiply_fusion), dimensions={1,2} | broadcast | bytes 40108032 | tf_op jit(solution)/shard_map/stack | solution.py:21
  25.8 8.0 all-to-all-start
  33.9 0.0 copy-start.1
  33.9 0.0 all-gather.2.cloned.1.call-start
  33.9 1.1 slice.4
  35.0 0.0 all-gather.2.cloned.1.call-update
  35.1 0.0 copy-done.1
  35.1 0.1 broadcast_bitcast_fusion
  35.2 0.3 broadcast_in_dim.16
  35.5 2.0 copy.8
  37.4 54.8 %all-gather.2.cloned.1.call-done = bf16[12288,384]{0,1:T(8,128)(2,1)} async-done(((bf16[1536,384]{0,1:T(8,128)(2,1)}), bf16[12288,384]{0,1:T(8,128)(2,1)}) %all-gather.2.cloned.1.call-update) | async-done | bytes 9437200 | tf_op jit(solution)/shard_map/all_gather | solution.py:18
  92.2 643.4 %all-to-all-done = bf16[16,1536,768]{1,2,0:T(8,128)(2,1)} async-done(((bf16[16,1536,768]{1,2,0:T(8,128)(2,1)}), bf16[16,1536,768]{1,2,0:T(8,128)(2,1)}, u32[]{:S(2)}, u32[]{:S(2)}) %all-to-all-start) | async-done | bytes 37748768 | tf_op jit(solution)/shard_map/all_to_all | solution.py:21
  735.6 27.0 %fusion.1 = (f32[384]{0:T(512)S(1)}, f32[384]{0:T(512)S(1)}, f32[384]{0:T(512)S(1)}, f32[1536,384]{1,0:T(8,128)S(1)}) fusion(f32[1536,384]{1,0:T(8,128)} %copy.8, bf16[1536,12288]{0,1:T(8,128)(2,1)} %bitcast.2, bf16[12288,384]{0,1:T(8,128)(2,1)} %all-gather.2.cloned.1.call-done), kind=kOutput, calls=%fused_computation.10 | convolution fusion | flops 14499053568 | bytes 51909120 | tf_op jit(solution)/shard_map/dot_general | solution.py:19
  762.7 14.0 %pmax.14 = f32[384]{0:T(512)S(1)} all-reduce(f32[384]{0:T(512)S(1)} %get-tuple-element.2), channel_id=1, replica_groups=mesh['row'=8,'col'=16] {'row'}, use_global_device_ids=true, to_apply=%region_3.0 | all-reduce | flops 384 | bytes 3072 | tf_op jit(solution)/shard_map/pmax | solution.py:34
  776.7 12.4 %all-reduce = (f32[384]{0:T(512)S(1)}, f32[384]{0:T(512)S(1)}) all-reduce(f32[384]{0:T(512)S(1)} %get-tuple-element.4, f32[384]{0:T(512)S(1)} %get-tuple-element.3), channel_id=1, replica_groups=mesh['row'=8,'col'=16] {'row'}, use_global_device_ids=true, to_apply=%region_1.0 | all-reduce | flops 768 | bytes 6144 | tf_op jit(solution)/shard_map/psum | solution.py:28
  789.1 0.6 subtract_reduce_fusion
  789.7 40.0 %pmax.15 = f32[]{:T(128)} all-reduce(f32[]{:T(128)} %subtract_reduce_fusion), channel_id=1, replica_groups=mesh['row'=8,'col'=16] {'col'}, use_global_device_ids=true, to_apply=%region_7.0 | all-reduce | flops 1 | bytes 8 | tf_op jit(solution)/shard_map/pmax | solution.py:36
  829.6 1.6 divide_multiply_fusion
  (4 shorter events, 0.0 us)
Async XLA Ops:
  7.2 4.3 copy-start
  25.8 709.8 %all-to-all-start = ((bf16[16,1536,768]{1,2,0:T(8,128)(2,1)}), bf16[16,1536,768]{1,2,0:T(8,128)(2,1)}, u32[]{:S(2)}, u32[]{:S(2)}) async-start(bf16[16,1536,768]{1,2,0:T(8,128)(2,1)} %stack.2), calls=%async_computation | async-start | bytes 75497472 | tf_op jit(solution)/shard_map/all_to_all | solution.py:21
  33.9 1.2 copy-start.1
  33.9 58.3 %all-gather.2.cloned.1.call-start = ((), (), s32[]{:S(2)}) async-start(), calls=%async_computation.1 | async-start | bytes 10616832 | tf_op jit(solution)/shard_map/all_gather | solution.py:18
Sparse Core Ops, SparseCore 0:
  36.4 55.7 all-gather.1
